TPU v7x, 256 devices: a whole 4x4x8 slice. The times are simulated.
256 devices in a mesh: seq: 16 (over y, x), ctx: 16 (over z, core).
Axes of the slice: x: 4, y: 4, z: 8, core: 2. Of those that a mesh axis runs over, the one named last changes fastest.
Arguments:
- queries: bfloat16 [16, 2048, 2048], P('ctx', 'seq'), may hold values from -30 to 30
- keys: bfloat16 [16, 2048, 2048], P('ctx', 'seq'), may hold values from -30 to 30
- values: bfloat16 [16, 2048, 2048], P('ctx', 'seq'), may hold values from -6 to 6
- out_grad: bfloat16 [16, 2048, 2048], P('ctx', 'seq'), may hold values from -6 to 6
- tile_mask: int32 [16, 16, 16, 256], P('seq'), may hold values from 0 to 1, as said below
Outputs:
- attended: bfloat16 [16, 2048, 2048], P('ctx', 'seq')
- query_grad: bfloat16 [16, 2048, 2048], P('ctx', 'seq')
- key_grad: bfloat16 [16, 2048, 2048], P('ctx', 'seq')
- value_grad: bfloat16 [16, 2048, 2048], P('ctx', 'seq')
Inputs may be any that keep to these rules, and one draw needn't show every extreme that they name: tile_mask[h, f, i, t] is 1 only where the key tile t lies in frame f - 1, f or f + 1; every query tile attends its own tile; a query tile attends at most 18 key tiles and some query tile attends exactly 18.
All inputs are finite; a program needn't handle non-finite values.
Results may differ from a plain program's by a relative error of at most 0.025.
Values may be sent and summed in bfloat16 or wider, within the bound.
A program may use at most 128 MiB of HBM per device.

v0:
```python
import functools

import jax
import jax.numpy as jnp
from jax import lax
from jax.experimental import pallas as pl
from jax.experimental.pallas import tpu as pltpu
from jax.sharding import PartitionSpec as P

MESH = pl.DeviceIdType.MESH
HD = 128
LOG2E = 1.4426950408889634
NEG = -1e30


def dot_nt(a, b):
    return lax.dot_general(a, b, (((1,), (1,)), ((), ())), preferred_element_type=jnp.float32)


def dot_nn(a, b):
    return lax.dot_general(a, b, (((1,), (0,)), ((), ())), preferred_element_type=jnp.float32)


def kernel(
    rows, cols, slots, groups, frames,
    ci, bias, gp, gq, keep, last,
    q_in, k_in, v_in, g_in,
    o_out, dq_out, dk_out, dv_out,
    k3, v3, qh, gh, sbuf, pst, dst, qt, gt, park, parv, ot, dqt, snd, rcv, dkt, dvt,
    in_send, in_recv, in_local, halo_send, halo_recv, gr_send, gr_recv, out_send, out_recv, out_local,
):
    n = rows * cols
    me = lax.axis_index("seq")
    frame = lax.axis_index("ctx")
    my_row, my_col = me // cols, me % cols
    has_prev, has_next = frame > 0, frame < frames - 1

    def peer(r, sign):
        dr, dc = r // cols, r % cols
        row = lax.rem(my_row + sign * dr + rows, rows)
        col = lax.rem(my_col + sign * dc + cols, cols)
        return row * cols + col

    barrier = pltpu.get_barrier_semaphore()

    def greet(r, _):
        pl.semaphore_signal(barrier, inc=1, device_id=(peer(r, 1), frame), device_id_type=MESH)
        return 0

    lax.fori_loop(1, n, greet, 0)

    for step in (1, frames - 1):
        beside = lax.rem(frame + step, frames)
        pl.semaphore_signal(barrier, inc=1, device_id=(me, beside), device_id_type=MESH)
    pl.semaphore_wait(barrier, n + 1)

    arrays = ((k_in, k3, n), (v_in, v3, n), (q_in, qh, 0), (g_in, gh, 0))

    def in_copy(a, target, source):
        src, dst_ref, base = arrays[a]
        return pltpu.make_async_remote_copy(
            src_ref=src.at[0, :, pl.ds(pl.multiple_of(target * HD, HD), HD)],
            dst_ref=dst_ref.at[base + source],
            send_sem=in_send.at[a, target],
            recv_sem=in_recv.at[a, source],
            device_id=(target, frame),
            device_id_type=MESH,
        )

    def in_own(a):
        src, dst_ref, base = arrays[a]
        return pltpu.make_async_copy(
            src.at[0, :, pl.ds(pl.multiple_of(me * HD, HD), HD)],
            dst_ref.at[base + me],
            in_local.at[a],
        )

    for a in range(4):
        in_own(a).start()

        def send(r, _, a=a):
            in_copy(a, peer(r, 1), me).start()
            return 0

        lax.fori_loop(1, n, send, 0)

    def halo_copy(a, side):
        ref = (k3, v3)[a]
        return pltpu.make_async_remote_copy(
            src_ref=ref.at[pl.ds(n, n)],
            dst_ref=ref.at[pl.ds(2 * n if side == 0 else 0, n)],
            send_sem=halo_send.at[a, side],
            recv_sem=halo_recv.at[a, side],
            device_id=(me, frame - 1 if side == 0 else frame + 1),
            device_id_type=MESH,
        )

    sides = ((0, has_prev, has_next), (1, has_next, has_prev))
    zero_tile = jnp.zeros((HD, HD), jnp.bfloat16)
    pst[n * slots] = zero_tile
    dst[n * slots] = zero_tile
    park[groups] = zero_tile
    parv[groups] = zero_tile

    @pl.when(jnp.logical_not(has_prev))
    def _():
        k3[0:n] = jnp.zeros((n, HD, HD), jnp.bfloat16)
        v3[0:n] = jnp.zeros((n, HD, HD), jnp.bfloat16)
        rcv[1] = jnp.zeros(rcv.shape[1:], jnp.bfloat16)

    @pl.when(jnp.logical_not(has_next))
    def _():
        k3[2 * n : 3 * n] = jnp.zeros((n, HD, HD), jnp.bfloat16)
        v3[2 * n : 3 * n] = jnp.zeros((n, HD, HD), jnp.bfloat16)
        rcv[0] = jnp.zeros(rcv.shape[1:], jnp.bfloat16)

    for a in range(2):
        in_own(a).wait()

        def arrive(r, _, a=a):
            in_copy(a, peer(r, 1), peer(r, -1)).wait_recv()
            return 0

        lax.fori_loop(1, n, arrive, 0)
        for side, send_if, _ in sides:
            @pl.when(send_if)
            def _(a=a, side=side):
                halo_copy(a, side).start()

    for a in range(2):
        for side, _, recv_if in sides:
            @pl.when(recv_if)
            def _(a=a, side=side):
                halo_copy(a, side).wait_recv()

    half = slots // 2
    scale = HD ** -0.5
    out_arrays = ((ot, o_out), (dqt, dq_out), (dkt, dk_out), (dvt, dv_out))

    def out_copy(a, target, source):
        tiles, out = out_arrays[a]
        return pltpu.make_async_remote_copy(
            src_ref=tiles.at[target],
            dst_ref=out.at[0, :, pl.ds(pl.multiple_of(source * HD, HD), HD)],
            send_sem=out_send.at[a, target],
            recv_sem=out_recv.at[a, source],
            device_id=(target, frame),
            device_id_type=MESH,
        )

    def out_own(a):
        tiles, out = out_arrays[a]
        return pltpu.make_async_copy(
            tiles.at[me],
            out.at[0, :, pl.ds(pl.multiple_of(me * HD, HD), HD)],
            out_local.at[a],
        )

    def pair_of(ref, i, jj):
        return jnp.concatenate([ref[ci[i, 2 * jj]], ref[ci[i, 2 * jj + 1]]], axis=0)

    def query_tile(i):
        q = qh[i]
        g = gh[i]
        gf = g.astype(jnp.float32)
        gt[i] = gf.T.astype(jnp.bfloat16)
        qt[i] = q.astype(jnp.float32).T.astype(jnp.bfloat16)
        top = jnp.full((HD, HD), NEG, jnp.float32)
        for jj in range(half):
            s = dot_nt(q, pair_of(k3, i, jj)) * (scale * LOG2E)
            s0 = s[:, :HD] + bias[i, 2 * jj]
            s1 = s[:, HD:] + bias[i, 2 * jj + 1]
            sbuf[:, jj * 2 * HD : jj * 2 * HD + HD] = s0
            sbuf[:, jj * 2 * HD + HD : (jj + 1) * 2 * HD] = s1
            top = jnp.maximum(top, jnp.maximum(s0, s1))
        highest = jnp.max(top, axis=1, keepdims=True)
        total = jnp.zeros((HD, HD), jnp.float32)
        o = jnp.zeros((HD, HD), jnp.float32)
        for jj in range(half):
            at = slice(jj * 2 * HD, (jj + 1) * 2 * HD)
            p = jnp.exp2(sbuf[:, at] - highest)
            sbuf[:, at] = p
            total = total + (p[:, :HD] + p[:, HD:])
            o = o + dot_nn(p.astype(jnp.bfloat16), pair_of(v3, i, jj))
        inv = 1.0 / jnp.sum(total, axis=1, keepdims=True)
        o = o * inv
        ob = o.astype(jnp.bfloat16)
        ot[i] = ob
        row_dot = jnp.sum(gf * ob.astype(jnp.float32), axis=1, keepdims=True)
        dq = jnp.zeros((HD, HD), jnp.float32)
        for jj in range(half):
            at = slice(jj * 2 * HD, (jj + 1) * 2 * HD)
            p = sbuf[:, at] * inv
            dp = dot_nt(g, pair_of(v3, i, jj))
            ds = (p * (dp - row_dot)).astype(jnp.bfloat16)
            pb = p.astype(jnp.bfloat16)
            dq = dq + dot_nn(ds, pair_of(k3, i, jj))
            base = i * slots + 2 * jj
            pst[base] = pb[:, :HD]
            pst[base + 1] = pb[:, HD:]
            dst[base] = ds[:, :HD]
            dst[base + 1] = ds[:, HD:]
        dqt[i] = (dq * scale).astype(jnp.bfloat16)

    def own_tile():
        for a in (2, 3):
            in_own(a).wait()
        query_tile(me)
        for a in (0, 1):
            out_own(a).start()

    def other_tile(r, _):
        source = peer(r, -1)
        for a in (2, 3):
            in_copy(a, peer(r, 1), source).wait_recv()
        query_tile(source)
        for a in (0, 1):
            out_copy(a, source, me).start()
        return 0

    own_tile()
    lax.fori_loop(1, n, other_tile, 0)

    def group(x, carry):
        acc_k, acc_v = carry
        a, b = gp[2 * x], gp[2 * x + 1]
        qa, qb = gq[2 * x], gq[2 * x + 1]
        hold = keep[x]
        acc_v = acc_v * hold + dot_nn(
            jnp.concatenate([gt[qa], gt[qb]], axis=1), jnp.concatenate([pst[a], pst[b]], axis=0))
        acc_k = acc_k * hold + dot_nn(
            jnp.concatenate([qt[qa], qt[qb]], axis=1), jnp.concatenate([dst[a], dst[b]], axis=0))
        parv[x] = acc_v.astype(jnp.bfloat16)
        park[x] = (acc_k * scale).astype(jnp.bfloat16)
        return acc_k, acc_v

    zero = jnp.zeros((HD, HD), jnp.float32)
    lax.fori_loop(0, groups, group, (zero, zero))

    def tile_of(par, t):
        return par[last[t]].astype(jnp.float32).T

    def gr_copy(a, side, i):
        return pltpu.make_async_remote_copy(
            src_ref=snd.at[side, a, i],
            dst_ref=rcv.at[side, a, i],
            send_sem=gr_send.at[side, a, i],
            recv_sem=gr_recv.at[side, a, i],
            device_id=(me, frame - 1 if side == 0 else frame + 1),
            device_id_type=MESH,
        )

    def neighbour_terms(i, _):
        for side, send_if, _ in sides:
            @pl.when(send_if)
            def _(side=side):
                for a in range(2):
                    t = i if side == 0 else 2 * n + i
                    snd[side, a, i] = tile_of((park, parv)[a], t).astype(jnp.bfloat16)
                    gr_copy(a, side, i).start()
        return 0

    lax.fori_loop(0, n, neighbour_terms, 0)

    def finish(i):
        for side, _, recv_if in sides:
            @pl.when(recv_if)
            def _(side=side):
                for a in range(2):
                    gr_copy(a, side, i).wait_recv()
        for a in range(2):
            tot = tile_of((park, parv)[a], n + i)
            tot = tot + rcv[0, a, i].astype(jnp.float32) + rcv[1, a, i].astype(jnp.float32)
            (dkt, dvt)[a][i] = tot.astype(jnp.bfloat16)

    def finish_other(r, _):
        i = peer(r, -1)
        finish(i)
        for a in (2, 3):
            out_copy(a, i, me).start()
        return 0

    lax.fori_loop(1, n, finish_other, 0)
    finish(me)
    for a in (2, 3):
        out_own(a).start()

    for a in range(4):
        out_own(a).wait()

        def settle(r, _, a=a):
            there, back = peer(r, 1), peer(r, -1)
            in_copy(a, there, me).wait_send()
            out_copy(a, back, me).wait_send()
            out_copy(a, there, back).wait_recv()
            return 0

        lax.fori_loop(1, n, settle, 0)
    for side, send_if, _ in sides:
        @pl.when(send_if)
        def _(side=side):
            for a in range(2):
                halo_copy(a, side).wait_send()

            def settle_terms(i, _):
                for a in range(2):
                    gr_copy(a, side, i).wait_send()
                return 0

            lax.fori_loop(0, n, settle_terms, 0)


def tables(window, slots, groups):
    n, total = window.shape
    w = window > 0
    t = jnp.arange(total, dtype=jnp.int32)
    i = jnp.arange(n, dtype=jnp.int32)
    before = (t[:, None] < t[None, :]).astype(jnp.int32)
    pos = jnp.sum(window[:, :, None] * before[None], axis=1)
    count = jnp.sum(window, axis=1)
    j = jnp.arange(slots, dtype=jnp.int32)
    hit = w[:, None, :] & (pos[:, None, :] == j[None, :, None])
    chosen = jnp.sum(jnp.where(hit, t[None, None, :], 0), axis=2)
    present = j[None, :] < count[:, None]
    chosen = jnp.where(present, chosen, n + i[:, None])
    bias = jnp.where(present, 0.0, NEG).astype(jnp.float32)
    pair = i[:, None] * slots + pos
    number = jnp.sum(window, axis=0)
    rank = jnp.sum(window[:, None, :] * (i[:, None, None] < i[None, :, None]).astype(jnp.int32), axis=0)
    used = (number + 1) // 2
    start = jnp.sum(used[:, None] * before, axis=0)
    place = jnp.where(w, 2 * start[None, :] + rank, -1)
    x = jnp.arange(2 * groups, dtype=jnp.int32)
    found = place.reshape(1, -1) == x[:, None]
    gp = jnp.sum(jnp.where(found, pair.reshape(1, -1) - n * slots, 0), axis=1) + n * slots
    gq = jnp.minimum(gp // slots, n - 1)
    opens = jnp.any((start[None, :] == jnp.arange(groups)[:, None]) & (number > 0)[None, :], axis=1)
    keep = jnp.where(opens, 0.0, 1.0).astype(jnp.float32)
    last = jnp.where(number > 0, start + used - 1, groups)
    return chosen, bias, gp, gq, keep, last


def body(shape, queries, keys, values, out_grad, tile_mask):
    rows, cols, frames = shape
    n = rows * cols
    slots = min(18, 3 * n)
    groups = (n * slots + 3 * n) // 2
    frame = lax.axis_index("ctx")
    padded = jnp.pad(tile_mask[0], ((0, 0), (0, 0), (n, n)))
    own = lax.dynamic_index_in_dim(padded, frame, 0, keepdims=False)
    window = lax.dynamic_slice_in_dim(own, frame * n, 3 * n, 1)
    lists = tables(window, slots, groups)
    smem = pl.BlockSpec(memory_space=pltpu.SMEM)
    any_ = pl.BlockSpec(memory_space=pl.ANY)
    tile = lambda *lead: pltpu.VMEM(lead + (HD, HD), jnp.bfloat16)
    dma = pltpu.SemaphoreType.DMA
    return pl.pallas_call(
        functools.partial(kernel, rows, cols, slots, groups, frames),
        out_shape=[jax.ShapeDtypeStruct(queries.shape, jnp.bfloat16)] * 4,
        in_specs=[smem] * 6 + [any_] * 4,
        out_specs=[any_] * 4,
        scratch_shapes=[
            tile(3 * n), tile(3 * n), tile(n), tile(n),
            pltpu.VMEM((HD, slots * HD), jnp.float32),
            tile(n * slots + 1), tile(n * slots + 1),
            tile(n), tile(n),
            tile(groups + 1), tile(groups + 1),
            tile(n), tile(n), tile(2, 2, n), tile(2, 2, n), tile(n), tile(n),
            dma((4, n)), dma((4, n)), dma((4,)),
            dma((2, 2)), dma((2, 2)),
            dma((2, 2, n)), dma((2, 2, n)),
            dma((4, n)), dma((4, n)), dma((4,)),
        ],
        compiler_params=pltpu.CompilerParams(
            collective_id=0, has_side_effects=True, vmem_limit_bytes=56 * 1024 * 1024),
    )(*lists, queries, keys, values, out_grad)


def solution(mesh):
    n, frames = mesh.shape["seq"], mesh.shape["ctx"]
    cols = 4 if n % 4 == 0 and n > 4 else 2
    shape = (n // cols, cols, frames)
    data = P("ctx", "seq", None)
    return jax.shard_map(
        functools.partial(body, shape),
        mesh=mesh,
        in_specs=(data,) * 4 + (P("seq", None, None, None),),
        out_specs=(data,) * 4,
        check_vma=False,
    )
```

profile of v0, /device:TPU:111, one launch (start us, length us, event | category | flops | bytes accessed | tf_op | source)
XLA Modules:
  0.0 128.8 jit_solution(13453287040911283310)
XLA Ops:
  0.7 0.8 broadcast_compare_fusion
  1.5 0.1 gt.33
  1.6 0.1 multiply_reduce_fusion.1
  1.7 0.1 fusion.9
  1.8 0.1 select_reduce_fusion.2
  1.9 0.1 fusion.2
  2.0 0.6 add_select_fusion.1
  2.6 0.1 add.85
  2.7 0.6 broadcast_select_fusion.1.keep
  3.3 0.7 fusion.4.bias
  3.9 0.2 multiply_reduce_fusion
  4.1 0.1 add_add_fusion
  4.2 0.1 sub.23
  4.3 0.2 select_reduce_fusion
  4.5 0.4 select_reduce_fusion.1
  4.9 0.1 copy.9
  4.9 0.7 fusion.5.ci
  5.6 0.6 fusion.7
  6.2 117.4 %shard_map.84 = (bf16[1,128,2048]{2,1,0:T(8,128)(2,1)}, bf16[1,128,2048]{2,1,0:T(8,128)(2,1)}, bf16[1,128,2048]{2,1,0:T(8,128)(2,1)}, bf16[1,128,2048]{2,1,0:T(8,128)(2,1)}) custom-call(s32[16,18]{1,0:T(8,128)} %fusion.5.ci, f32[16,18]{1,0:T(8,128)} %fusion.4.bias, s32[336]{0:T(512)} %get-tuple-element.9.gp, s32[336]{0:T(512)} %get-tuple-element.8.gq, ...), custom_call_target="tpu_custom_call" | custom-call | tf_op jit(solution)/shard_map/pallas_call | solution.py:357
  123.6 0.0 copy-start.2
  123.6 1.9 %copy.14 = bf16[1,128,2048]{2,1,0:T(8,128)(2,1)} copy(bf16[1,128,2048]{2,1,0:T(8,128)(2,1)} %get-tuple-element.16) | data formatting | bytes 1048576
  125.5 0.0 copy-done.2
  125.5 0.0 copy-start.1
  125.6 0.8 copy.15
  126.3 0.4 copy-done.1
  126.8 0.0 copy-start
  126.8 0.8 copy.16
  127.6 0.4 copy-done
  128.0 0.8 copy.17
  (9 shorter events, 0.0 us)
Async XLA Ops:
  123.6 2.0 %copy-start.2 = (bf16[1,128,2048]{2,1,0:T(8,128)(2,1)S(1)}, bf16[1,128,2048]{2,1,0:T(8,128)(2,1)}, u32[]{:S(2)}) copy-start(bf16[1,128,2048]{2,1,0:T(8,128)(2,1)} %get-tuple-element.17) | copy-start | bytes 1572868
  125.5 1.2 copy-start.1
  126.8 1.2 copy-start
where the time goes:
time: 129 us
  Pallas kernels  117 us (91%)
  local copies, waits for them, and re-layouts  5.52 us (4%)
  other arithmetic  5.2 us (4%)
    pallas_call x1, Pallas kernels, body(): pl.pallas_call(functools.partial(kernel, rows, cols, slots, groups, frame...  117 us
    unnamed x10, local copies, waits for them, and re-layouts  5.19 us

commit v1 on v0

--- a/solution.py
+++ b/solution.py
@@ -11,6 +11,7 @@
 HD = 128
 LOG2E = 1.4426950408889634
 NEG = -1e30
+BLOCK = 4
 
 
 def dot_nt(a, b):
@@ -19,6 +20,14 @@
 
 def dot_nn(a, b):
     return lax.dot_general(a, b, (((1,), (0,)), ((), ())), preferred_element_type=jnp.float32)
+
+
+def together(*parts):
+    parts = list(parts)
+    while parts:
+        for part in list(parts):
+            if next(part, True):
+                parts.remove(part)
 
 
 def kernel(
@@ -84,13 +93,14 @@
 
         lax.fori_loop(1, n, send, 0)
 
-    def halo_copy(a, side):
+    def halo_copy(a, side, chunk):
         ref = (k3, v3)[a]
+        first = chunk * cols
         return pltpu.make_async_remote_copy(
-            src_ref=ref.at[pl.ds(n, n)],
-            dst_ref=ref.at[pl.ds(2 * n if side == 0 else 0, n)],
-            send_sem=halo_send.at[a, side],
-            recv_sem=halo_recv.at[a, side],
+            src_ref=ref.at[pl.ds(n + first, cols)],
+            dst_ref=ref.at[pl.ds((2 * n if side == 0 else 0) + first, cols)],
+            send_sem=halo_send.at[a, side, chunk],
+            recv_sem=halo_recv.at[a, side, chunk],
             device_id=(me, frame - 1 if side == 0 else frame + 1),
             device_id_type=MESH,
         )
@@ -116,22 +126,23 @@
 
     for a in range(2):
         in_own(a).wait()
-
-        def arrive(r, _, a=a):
-            in_copy(a, peer(r, 1), peer(r, -1)).wait_recv()
-            return 0
-
-        lax.fori_loop(1, n, arrive, 0)
-        for side, send_if, _ in sides:
-            @pl.when(send_if)
-            def _(a=a, side=side):
-                halo_copy(a, side).start()
+        for dr in range(rows):
+            for dc in range(cols):
+                r = dr * cols + dc
+                if r > 0:
+                    in_copy(a, peer(r, 1), peer(r, -1)).wait_recv()
+            chunk = lax.rem(my_row - dr + rows, rows)
+            for side, send_if, _ in sides:
+                @pl.when(send_if)
+                def _(a=a, side=side, chunk=chunk):
+                    halo_copy(a, side, chunk).start()
 
     for a in range(2):
         for side, _, recv_if in sides:
             @pl.when(recv_if)
             def _(a=a, side=side):
-                halo_copy(a, side).wait_recv()
+                for chunk in range(rows):
+                    halo_copy(a, side, chunk).wait_recv()
 
     half = slots // 2
     scale = HD ** -0.5
@@ -159,86 +170,125 @@
     def pair_of(ref, i, jj):
         return jnp.concatenate([ref[ci[i, 2 * jj]], ref[ci[i, 2 * jj + 1]]], axis=0)
 
-    def query_tile(i):
-        q = qh[i]
-        g = gh[i]
-        gf = g.astype(jnp.float32)
-        gt[i] = gf.T.astype(jnp.bfloat16)
-        qt[i] = q.astype(jnp.float32).T.astype(jnp.bfloat16)
-        top = jnp.full((HD, HD), NEG, jnp.float32)
-        for jj in range(half):
-            s = dot_nt(q, pair_of(k3, i, jj)) * (scale * LOG2E)
-            s0 = s[:, :HD] + bias[i, 2 * jj]
-            s1 = s[:, HD:] + bias[i, 2 * jj + 1]
-            sbuf[:, jj * 2 * HD : jj * 2 * HD + HD] = s0
-            sbuf[:, jj * 2 * HD + HD : (jj + 1) * 2 * HD] = s1
-            top = jnp.maximum(top, jnp.maximum(s0, s1))
-        highest = jnp.max(top, axis=1, keepdims=True)
-        total = jnp.zeros((HD, HD), jnp.float32)
-        o = jnp.zeros((HD, HD), jnp.float32)
-        for jj in range(half):
-            at = slice(jj * 2 * HD, (jj + 1) * 2 * HD)
-            p = jnp.exp2(sbuf[:, at] - highest)
-            sbuf[:, at] = p
-            total = total + (p[:, :HD] + p[:, HD:])
-            o = o + dot_nn(p.astype(jnp.bfloat16), pair_of(v3, i, jj))
-        inv = 1.0 / jnp.sum(total, axis=1, keepdims=True)
-        o = o * inv
-        ob = o.astype(jnp.bfloat16)
-        ot[i] = ob
-        row_dot = jnp.sum(gf * ob.astype(jnp.float32), axis=1, keepdims=True)
-        dq = jnp.zeros((HD, HD), jnp.float32)
-        for jj in range(half):
-            at = slice(jj * 2 * HD, (jj + 1) * 2 * HD)
-            p = sbuf[:, at] * inv
-            dp = dot_nt(g, pair_of(v3, i, jj))
-            ds = (p * (dp - row_dot)).astype(jnp.bfloat16)
-            pb = p.astype(jnp.bfloat16)
-            dq = dq + dot_nn(ds, pair_of(k3, i, jj))
-            base = i * slots + 2 * jj
-            pst[base] = pb[:, :HD]
-            pst[base + 1] = pb[:, HD:]
-            dst[base] = ds[:, :HD]
-            dst[base + 1] = ds[:, HD:]
-        dqt[i] = (dq * scale).astype(jnp.bfloat16)
-
-    def own_tile():
-        for a in (2, 3):
-            in_own(a).wait()
-        query_tile(me)
-        for a in (0, 1):
-            out_own(a).start()
-
-    def other_tile(r, _):
-        source = peer(r, -1)
-        for a in (2, 3):
-            in_copy(a, peer(r, 1), source).wait_recv()
-        query_tile(source)
-        for a in (0, 1):
-            out_copy(a, source, me).start()
+    def query_phases(i, logits):
+        held = {}
+
+        def scores():
+            q = qh[i]
+            gt[i] = gh[i].astype(jnp.float32).T.astype(jnp.bfloat16)
+            qt[i] = q.astype(jnp.float32).T.astype(jnp.bfloat16)
+            top = jnp.full((HD, HD), NEG, jnp.float32)
+            for jj in range(half):
+                s = dot_nt(q, pair_of(k3, i, jj)) * (scale * LOG2E)
+                s0 = s[:, :HD] + bias[i, 2 * jj]
+                s1 = s[:, HD:] + bias[i, 2 * jj + 1]
+                logits[:, jj * 2 * HD : jj * 2 * HD + HD] = s0
+                logits[:, jj * 2 * HD + HD : (jj + 1) * 2 * HD] = s1
+                top = jnp.maximum(top, jnp.maximum(s0, s1))
+                yield
+            held["highest"] = jnp.max(top, axis=1, keepdims=True)
+
+        def output():
+            highest = held["highest"]
+            total = jnp.zeros((HD, HD), jnp.float32)
+            o = jnp.zeros((HD, HD), jnp.float32)
+            for jj in range(half):
+                at = slice(jj * 2 * HD, (jj + 1) * 2 * HD)
+                p = jnp.exp2(logits[:, at] - highest)
+                logits[:, at] = p
+                total = total + (p[:, :HD] + p[:, HD:])
+                o = o + dot_nn(p.astype(jnp.bfloat16), pair_of(v3, i, jj))
+                yield
+            inv = 1.0 / jnp.sum(total, axis=1, keepdims=True)
+            ob = (o * inv).astype(jnp.bfloat16)
+            ot[i] = ob
+            held["inv"] = inv
+            held["row_dot"] = jnp.sum(
+                gh[i].astype(jnp.float32) * ob.astype(jnp.float32), axis=1, keepdims=True)
+
+        def gradients():
+            g, inv, row_dot = gh[i], held["inv"], held["row_dot"]
+            dq = jnp.zeros((HD, HD), jnp.float32)
+            for jj in range(half):
+                at = slice(jj * 2 * HD, (jj + 1) * 2 * HD)
+                p = logits[:, at] * inv
+                dp = dot_nt(g, pair_of(v3, i, jj))
+                ds = (p * (dp - row_dot)).astype(jnp.bfloat16)
+                pb = p.astype(jnp.bfloat16)
+                dq = dq + dot_nn(ds, pair_of(k3, i, jj))
+                base = i * slots + 2 * jj
+                pst[base] = pb[:, :HD]
+                pst[base + 1] = pb[:, HD:]
+                dst[base] = ds[:, :HD]
+                dst[base + 1] = ds[:, HD:]
+                yield
+            dqt[i] = (dq * scale).astype(jnp.bfloat16)
+
+        return scores, output, gradients
+
+    def query_block(b, _):
+        tiles = [peer(b * BLOCK + u, -1) for u in range(BLOCK)]
+        for u in range(BLOCK):
+            r = b * BLOCK + u
+
+            def came(r=r, u=u):
+                for a in (2, 3):
+                    in_copy(a, peer(r, 1), tiles[u]).wait_recv()
+
+            if u > 0:
+                came()
+            else:
+                pl.when(b > 0)(came)
+
+                @pl.when(b == 0)
+                def _():
+                    for a in (2, 3):
+                        in_own(a).wait()
+
+        steps = [query_phases(tiles[u], sbuf.at[u]) for u in range(BLOCK)]
+        together(steps[0][0]())
+        for u in range(BLOCK):
+            if u + 1 < BLOCK:
+                together(steps[u][1](), steps[u + 1][0]())
+                together(steps[u][2]())
+            else:
+                together(steps[u][1]())
+                together(steps[u][2]())
+        for u in range(BLOCK):
+
+            def leave(u=u):
+                for a in (0, 1):
+                    out_copy(a, tiles[u], me).start()
+
+            if u > 0:
+                leave()
+            else:
+                pl.when(b > 0)(leave)
+
+                @pl.when(b == 0)
+                def _():
+                    for a in (0, 1):
+                        out_own(a).start()
         return 0
 
-    own_tile()
-    lax.fori_loop(1, n, other_tile, 0)
-
-    def group(x, carry):
-        acc_k, acc_v = carry
-        a, b = gp[2 * x], gp[2 * x + 1]
-        qa, qb = gq[2 * x], gq[2 * x + 1]
-        hold = keep[x]
-        acc_v = acc_v * hold + dot_nn(
-            jnp.concatenate([gt[qa], gt[qb]], axis=1), jnp.concatenate([pst[a], pst[b]], axis=0))
-        acc_k = acc_k * hold + dot_nn(
-            jnp.concatenate([qt[qa], qt[qb]], axis=1), jnp.concatenate([dst[a], dst[b]], axis=0))
-        parv[x] = acc_v.astype(jnp.bfloat16)
-        park[x] = (acc_k * scale).astype(jnp.bfloat16)
-        return acc_k, acc_v
-
-    zero = jnp.zeros((HD, HD), jnp.float32)
-    lax.fori_loop(0, groups, group, (zero, zero))
-
-    def tile_of(par, t):
-        return par[last[t]].astype(jnp.float32).T
+    lax.fori_loop(0, n // BLOCK, query_block, 0)
+
+    def key_side(a):
+        left, right, par = ((qt, dst, park), (gt, pst, parv))[a]
+
+        def group(x, acc):
+            one, two = gp[2 * x], gp[2 * x + 1]
+            term = dot_nn(
+                jnp.concatenate([left[gq[2 * x]], left[gq[2 * x + 1]]], axis=1),
+                jnp.concatenate([right[one], right[two]], axis=0))
+            acc = acc * keep[x] + term
+            par[x] = (acc * scale if a == 0 else acc).astype(jnp.bfloat16)
+            return acc
+
+        lax.fori_loop(0, groups, group, jnp.zeros((HD, HD), jnp.float32), unroll=12)
+
+    def tile_of(a, t):
+        return (park, parv)[a][last[t]].T
 
     def gr_copy(a, side, i):
         return pltpu.make_async_remote_copy(
@@ -250,40 +300,55 @@
             device_id_type=MESH,
         )
 
-    def neighbour_terms(i, _):
-        for side, send_if, _ in sides:
-            @pl.when(send_if)
-            def _(side=side):
-                for a in range(2):
-                    t = i if side == 0 else 2 * n + i
-                    snd[side, a, i] = tile_of((park, parv)[a], t).astype(jnp.bfloat16)
-                    gr_copy(a, side, i).start()
-        return 0
-
-    lax.fori_loop(0, n, neighbour_terms, 0)
-
-    def finish(i):
-        for side, _, recv_if in sides:
-            @pl.when(recv_if)
-            def _(side=side):
-                for a in range(2):
-                    gr_copy(a, side, i).wait_recv()
-        for a in range(2):
-            tot = tile_of((park, parv)[a], n + i)
-            tot = tot + rcv[0, a, i].astype(jnp.float32) + rcv[1, a, i].astype(jnp.float32)
-            (dkt, dvt)[a][i] = tot.astype(jnp.bfloat16)
-
-    def finish_other(r, _):
-        i = peer(r, -1)
-        finish(i)
-        for a in (2, 3):
-            out_copy(a, i, me).start()
-        return 0
-
-    lax.fori_loop(1, n, finish_other, 0)
-    finish(me)
-    for a in (2, 3):
-        out_own(a).start()
+    def neighbour_terms(a):
+        def four(b, _):
+            for side, send_if, _ in sides:
+                @pl.when(send_if)
+                def _(side=side):
+                    for u in range(BLOCK):
+                        i = b * BLOCK + u
+                        snd[side, a, i] = tile_of(a, i if side == 0 else 2 * n + i)
+                    for u in range(BLOCK):
+                        gr_copy(a, side, b * BLOCK + u).start()
+            return 0
+
+        lax.fori_loop(0, n // BLOCK, four, 0)
+
+    def finish(a):
+        def four(b, _):
+            tiles = [peer(b * BLOCK + u, -1) for u in range(BLOCK)]
+            for side, _, recv_if in sides:
+                @pl.when(recv_if)
+                def _(side=side):
+                    for i in tiles:
+                        gr_copy(a, side, i).wait_recv()
+            for i in tiles:
+                tot = tile_of(a, n + i).astype(jnp.float32)
+                tot = tot + rcv[0, a, i].astype(jnp.float32) + rcv[1, a, i].astype(jnp.float32)
+                (dkt, dvt)[a][i] = tot.astype(jnp.bfloat16)
+            for u, i in enumerate(tiles):
+
+                def leave(i=i):
+                    out_copy(2 + a, i, me).start()
+
+                if u > 0:
+                    leave()
+                else:
+                    pl.when(b > 0)(leave)
+
+                    @pl.when(b == 0)
+                    def _():
+                        out_own(2 + a).start()
+            return 0
+
+        lax.fori_loop(0, n // BLOCK, four, 0)
+
+    key_side(1)
+    neighbour_terms(1)
+    key_side(0)
+    neighbour_terms(0)
+    finish(1)
+    finish(0)
 
     for a in range(4):
         out_own(a).wait()
@@ -300,7 +365,8 @@
         @pl.when(send_if)
         def _(side=side):
             for a in range(2):
-                halo_copy(a, side).wait_send()
+                for chunk in range(rows):
+                    halo_copy(a, side, chunk).wait_send()
 
             def settle_terms(i, _):
                 for a in range(2):
@@ -361,13 +427,13 @@
         out_specs=[any_] * 4,
         scratch_shapes=[
             tile(3 * n), tile(3 * n), tile(n), tile(n),
-            pltpu.VMEM((HD, slots * HD), jnp.float32),
+            pltpu.VMEM((BLOCK, HD, slots * HD), jnp.float32),
             tile(n * slots + 1), tile(n * slots + 1),
             tile(n), tile(n),
             tile(groups + 1), tile(groups + 1),
             tile(n), tile(n), tile(2, 2, n), tile(2, 2, n), tile(n), tile(n),
             dma((4, n)), dma((4, n)), dma((4,)),
-            dma((2, 2)), dma((2, 2)),
+            dma((2, 2, rows)), dma((2, 2, rows)),
             dma((2, 2, n)), dma((2, 2, n)),
             dma((4, n)), dma((4, n)), dma((4,)),
         ],

time: 129 us -> 91.3 us (0.71)
  the two profiles are of different devices: /device:TPU:111 before, /device:TPU:129 now
where the time goes in v1:
time: 91.3 us; the launch traced here: 91 us
  Pallas kernels  79.6 us (87%)
  local copies, waits for them, and re-layouts  5.52 us (6%)
  other arithmetic  5.18 us (6%)
    pallas_call x1, Pallas kernels, body(): pl.pallas_call(functools.partial(kernel, rows, cols, slots, groups, frame...  79.6 us
    unnamed x10, local copies, waits for them, and re-layouts  5.19 us

profile of v1, /device:TPU:129, one launch (start us, length us, event | category | flops | bytes accessed | tf_op | source)
XLA Modules:
  0.0 91.0 jit_solution(7216003988311202749)
XLA Ops:
  0.7 0.8 broadcast_compare_fusion
  1.5 0.1 gt.33
  1.5 0.1 multiply_reduce_fusion.1
  1.7 0.1 fusion.9
  1.8 0.1 select_reduce_fusion.2
  1.9 0.1 fusion.2
  2.0 0.6 add_select_fusion.1
  2.6 0.1 add.85
  2.6 0.6 broadcast_select_fusion.1.keep
  3.2 0.7 fusion.4.bias
  3.9 0.2 multiply_reduce_fusion
  4.1 0.1 add_add_fusion
  4.2 0.1 sub.23
  4.3 0.2 select_reduce_fusion
  4.5 0.4 select_reduce_fusion.1
  4.8 0.1 copy.9
  4.9 0.7 fusion.5.ci
  5.6 0.6 fusion.7
  6.2 79.6 %shard_map.84 = (bf16[1,128,2048]{2,1,0:T(8,128)(2,1)}, bf16[1,128,2048]{2,1,0:T(8,128)(2,1)}, bf16[1,128,2048]{2,1,0:T(8,128)(2,1)}, bf16[1,128,2048]{2,1,0:T(8,128)(2,1)}) custom-call(s32[16,18]{1,0:T(8,128)} %fusion.5.ci, f32[16,18]{1,0:T(8,128)} %fusion.4.bias, s32[336]{0:T(512)} %get-tuple-element.9.gp, s32[336]{0:T(512)} %get-tuple-element.8.gq, ...), custom_call_target="tpu_custom_call" | custom-call | tf_op jit(solution)/shard_map/pallas_call | solution.py:423
  85.8 0.0 copy-start.2
  85.8 1.9 %copy.14 = bf16[1,128,2048]{2,1,0:T(8,128)(2,1)} copy(bf16[1,128,2048]{2,1,0:T(8,128)(2,1)} %get-tuple-element.16) | data formatting | bytes 1048576
  87.7 0.0 copy-done.2
  87.7 0.0 copy-start.1
  87.7 0.8 copy.15
  88.5 0.4 copy-done.1
  89.0 0.0 copy-start
  89.0 0.8 copy.16
  89.8 0.4 copy-done
  90.2 0.8 copy.17
  (9 shorter events, 0.1 us)
Async XLA Ops:
  85.8 2.0 %copy-start.2 = (bf16[1,128,2048]{2,1,0:T(8,128)(2,1)S(1)}, bf16[1,128,2048]{2,1,0:T(8,128)(2,1)}, u32[]{:S(2)}) copy-start(bf16[1,128,2048]{2,1,0:T(8,128)(2,1)} %get-tuple-element.17) | copy-start | bytes 1572868
  87.7 1.2 %copy-start.1 = (bf16[1,128,2048]{2,1,0:T(8,128)(2,1)S(1)}, bf16[1,128,2048]{2,1,0:T(8,128)(2,1)}, u32[]{:S(2)}) copy-start(bf16[1,128,2048]{2,1,0:T(8,128)(2,1)} %get-tuple-element.18) | copy-start | bytes 1572868
  89.0 1.2 %copy-start = (bf16[1,128,2048]{2,1,0:T(8,128)(2,1)S(1)}, bf16[1,128,2048]{2,1,0:T(8,128)(2,1)}, u32[]{:S(2)}) copy-start(bf16[1,128,2048]{2,1,0:T(8,128)(2,1)} %get-tuple-element.19) | copy-start | bytes 1572868

commit v2 on v1

--- a/solution.py
+++ b/solution.py
@@ -30,12 +30,60 @@
                 parts.remove(part)
 
 
+def build_tables(mask, frame, slots, groups, tables):
+    chosen, pairs, owners, last, bias, hold = tables
+    n, total = mask.shape
+    lines = pairs.shape[0]
+    iota = lambda dims, at: lax.broadcasted_iota(jnp.int32, dims, at)
+    flag = lambda x: jnp.where(x, 1.0, 0.0).astype(jnp.bfloat16)
+    w = mask[...]
+    wf = w.astype(jnp.float32)
+    wb = wf.astype(jnp.bfloat16)
+    before = flag(iota((total, total), 0) < iota((total, total), 1))
+    pos = dot_nn(wb, before)
+    count = jnp.sum(wf, axis=1, keepdims=True)
+    lane = iota((n, HD), 1)
+    tile = (iota((n, total), 1) - (frame - 1) * n).astype(jnp.float32)
+    own = (n + iota((n, 1), 0)).astype(jnp.float32)
+    row = jnp.zeros((n, HD), jnp.float32)
+    for j in range(slots):
+        here = jnp.sum(jnp.where((w > 0) & (pos == j), tile, 0.0), axis=1, keepdims=True)
+        here = jnp.where(count > j, here, own)
+        row = jnp.where(lane == j, here, row)
+    chosen[...] = row.astype(jnp.int32)
+    bias[...] = jnp.where(lane.astype(jnp.float32) < count, 0.0, NEG)
+    rank = dot_nn(flag(iota((n, n), 0) > iota((n, n), 1)), wb)
+    number = jnp.sum(w, axis=0, keepdims=True)
+    used = lax.shift_right_logical(number + 1, 1)
+    start = dot_nn(jnp.broadcast_to(used, (8, total)).astype(jnp.float32).astype(jnp.bfloat16), before)
+    final = jnp.where(number > 0, start.astype(jnp.int32) + used - 1, groups)
+    last[...] = final
+    place = jnp.where(w > 0, (2.0 * start[0:1] + rank).astype(jnp.int32), -16)
+    line, at = lax.shift_right_arithmetic(place, 4), place & 15
+    opens = jnp.where(rank == 0, 1.0, 0.0)
+    pair_of = jnp.full((lines, 16), n * slots, jnp.float32)
+    owner_of = jnp.zeros((lines, 16), jnp.float32)
+    opens_of = jnp.zeros((lines, 16), jnp.float32)
+    for i in range(n):
+        left = flag(iota((lines, total), 0) == line[i : i + 1])
+        right = jnp.where(iota((16, total), 0) == at[i : i + 1], 1.0, 0.0)
+        both = jnp.concatenate([right, right * pos[i : i + 1], right * opens[i : i + 1]], axis=0)
+        found = dot_nt(left, both.astype(jnp.bfloat16))
+        pair_of = pair_of + found[:, :16] * ((i - n) * slots) + found[:, 16:32]
+        owner_of = owner_of + found[:, :16] * i
+        opens_of = opens_of + found[:, 32:48]
+    wide = lambda x: jnp.concatenate([x, jnp.zeros((lines, HD - 16), jnp.float32)], axis=1)
+    pairs[...] = wide(pair_of).astype(jnp.int32)
+    owners[...] = wide(owner_of).astype(jnp.int32)
+    hold[...] = 1.0 - wide(opens_of)
+
+
 def kernel(
     rows, cols, slots, groups, frames,
-    ci, bias, gp, gq, keep, last,
-    q_in, k_in, v_in, g_in,
+    q_in, k_in, v_in, g_in, mask_in,
     o_out, dq_out, dk_out, dv_out,
     k3, v3, qh, gh, sbuf, pst, dst, qt, gt, park, parv, ot, dqt, snd, rcv, dkt, dvt,
+    mask, ci_v, gp_v, gq_v, last_v, bias_v, hold_v, ci, gp, gq, last, bias, hold, mask_sem, table_sem,
     in_send, in_recv, in_local, halo_send, halo_recv, gr_send, gr_recv, out_send, out_recv, out_local,
 ):
     n = rows * cols
@@ -50,6 +98,8 @@
         col = lax.rem(my_col + sign * dc + cols, cols)
         return row * cols + col
 
+    mask_copy = pltpu.make_async_copy(mask_in.at[0, frame], mask, mask_sem)
+    mask_copy.start()
     barrier = pltpu.get_barrier_semaphore()
 
     def greet(r, _):
@@ -106,6 +156,15 @@
         )
 
     sides = ((0, has_prev, has_next), (1, has_next, has_prev))
+    mask_copy.wait()
+    build_tables(mask, frame, slots, groups, (ci_v, gp_v, gq_v, last_v, bias_v, hold_v))
+    moves = [
+        pltpu.make_async_copy(built, table, table_sem.at[at])
+        for at, (built, table) in enumerate(
+            zip((ci_v, gp_v, gq_v, last_v, bias_v, hold_v), (ci, gp, gq, last, bias, hold)))
+    ]
+    for move in moves:
+        move.start()
     zero_tile = jnp.zeros((HD, HD), jnp.bfloat16)
     pst[n * slots] = zero_tile
     dst[n * slots] = zero_tile
@@ -123,6 +182,9 @@
         k3[2 * n : 3 * n] = jnp.zeros((n, HD, HD), jnp.bfloat16)
         v3[2 * n : 3 * n] = jnp.zeros((n, HD, HD), jnp.bfloat16)
         rcv[0] = jnp.zeros(rcv.shape[1:], jnp.bfloat16)
+
+    for move in moves:
+        move.wait()
 
     for a in range(2):
         in_own(a).wait()
@@ -167,8 +229,12 @@
             out_local.at[a],
         )
 
+    def within(at, size):
+        return jnp.minimum(jnp.maximum(at, 0), size - 1)
+
     def pair_of(ref, i, jj):
-        return jnp.concatenate([ref[ci[i, 2 * jj]], ref[ci[i, 2 * jj + 1]]], axis=0)
+        one, two = within(ci[i, 2 * jj], 3 * n), within(ci[i, 2 * jj + 1], 3 * n)
+        return jnp.concatenate([ref[one], ref[two]], axis=0)
 
     def query_phases(i, logits):
         held = {}
@@ -276,19 +342,23 @@
     def key_side(a):
         left, right, par = ((qt, dst, park), (gt, pst, parv))[a]
 
-        def group(x, acc):
-            one, two = gp[2 * x], gp[2 * x + 1]
-            term = dot_nn(
-                jnp.concatenate([left[gq[2 * x]], left[gq[2 * x + 1]]], axis=1),
-                jnp.concatenate([right[one], right[two]], axis=0))
-            acc = acc * keep[x] + term
-            par[x] = (acc * scale if a == 0 else acc).astype(jnp.bfloat16)
+        def row(y, acc):
+            for u in range(8):
+                whose = [within(gq[y, 2 * u + k], n) for k in range(2)]
+                which = [within(gp[y, 2 * u + k], n * slots + 1) for k in range(2)]
+                term = dot_nn(
+                    jnp.concatenate([left[k] for k in whose], axis=1),
+                    jnp.concatenate([right[k] for k in which], axis=0))
+                acc = acc * hold[y, 2 * u] + term
+                par[8 * y + u] = (acc * scale if a == 0 else acc).astype(jnp.bfloat16)
             return acc
 
-        lax.fori_loop(0, groups, group, jnp.zeros((HD, HD), jnp.float32), unroll=12)
+        lines = groups // 8
+        unroll = 3 if lines % 3 == 0 else 1
+        lax.fori_loop(0, lines, row, jnp.zeros((HD, HD), jnp.float32), unroll=unroll)
 
     def tile_of(a, t):
-        return (park, parv)[a][last[t]].T
+        return (park, parv)[a][within(last[0, (frame - 1) * n + t], groups + 1)].T
 
     def gr_copy(a, side, i):
         return pltpu.make_async_remote_copy(
@@ -376,54 +446,22 @@
             lax.fori_loop(0, n, settle_terms, 0)
 
 
-def tables(window, slots, groups):
-    n, total = window.shape
-    w = window > 0
-    t = jnp.arange(total, dtype=jnp.int32)
-    i = jnp.arange(n, dtype=jnp.int32)
-    before = (t[:, None] < t[None, :]).astype(jnp.int32)
-    pos = jnp.sum(window[:, :, None] * before[None], axis=1)
-    count = jnp.sum(window, axis=1)
-    j = jnp.arange(slots, dtype=jnp.int32)
-    hit = w[:, None, :] & (pos[:, None, :] == j[None, :, None])
-    chosen = jnp.sum(jnp.where(hit, t[None, None, :], 0), axis=2)
-    present = j[None, :] < count[:, None]
-    chosen = jnp.where(present, chosen, n + i[:, None])
-    bias = jnp.where(present, 0.0, NEG).astype(jnp.float32)
-    pair = i[:, None] * slots + pos
-    number = jnp.sum(window, axis=0)
-    rank = jnp.sum(window[:, None, :] * (i[:, None, None] < i[None, :, None]).astype(jnp.int32), axis=0)
-    used = (number + 1) // 2
-    start = jnp.sum(used[:, None] * before, axis=0)
-    place = jnp.where(w, 2 * start[None, :] + rank, -1)
-    x = jnp.arange(2 * groups, dtype=jnp.int32)
-    found = place.reshape(1, -1) == x[:, None]
-    gp = jnp.sum(jnp.where(found, pair.reshape(1, -1) - n * slots, 0), axis=1) + n * slots
-    gq = jnp.minimum(gp // slots, n - 1)
-    opens = jnp.any((start[None, :] == jnp.arange(groups)[:, None]) & (number > 0)[None, :], axis=1)
-    keep = jnp.where(opens, 0.0, 1.0).astype(jnp.float32)
-    last = jnp.where(number > 0, start + used - 1, groups)
-    return chosen, bias, gp, gq, keep, last
-
-
 def body(shape, queries, keys, values, out_grad, tile_mask):
     rows, cols, frames = shape
     n = rows * cols
     slots = min(18, 3 * n)
-    groups = (n * slots + 3 * n) // 2
-    frame = lax.axis_index("ctx")
-    padded = jnp.pad(tile_mask[0], ((0, 0), (0, 0), (n, n)))
-    own = lax.dynamic_index_in_dim(padded, frame, 0, keepdims=False)
-    window = lax.dynamic_slice_in_dim(own, frame * n, 3 * n, 1)
-    lists = tables(window, slots, groups)
-    smem = pl.BlockSpec(memory_space=pltpu.SMEM)
+    groups = -(-(n * slots + 3 * n) // 16) * 8
+    lines = -(-groups // 256) * 32
     any_ = pl.BlockSpec(memory_space=pl.ANY)
     tile = lambda *lead: pltpu.VMEM(lead + (HD, HD), jnp.bfloat16)
     dma = pltpu.SemaphoreType.DMA
+    table_shapes = (
+        ((n, HD), jnp.int32), ((lines, HD), jnp.int32), ((lines, HD), jnp.int32),
+        ((8, frames * n), jnp.int32), ((n, HD), jnp.float32), ((lines, HD), jnp.float32))
     return pl.pallas_call(
         functools.partial(kernel, rows, cols, slots, groups, frames),
         out_shape=[jax.ShapeDtypeStruct(queries.shape, jnp.bfloat16)] * 4,
-        in_specs=[smem] * 6 + [any_] * 4,
+        in_specs=[any_] * 5,
         out_specs=[any_] * 4,
         scratch_shapes=[
             tile(3 * n), tile(3 * n), tile(n), tile(n),
@@ -432,6 +470,10 @@
             tile(n), tile(n),
             tile(groups + 1), tile(groups + 1),
             tile(n), tile(n), tile(2, 2, n), tile(2, 2, n), tile(n), tile(n),
+            pltpu.VMEM((n, frames * n), jnp.int32),
+            *[pltpu.VMEM(dims, kind) for dims, kind in table_shapes],
+            *[pltpu.SMEM(dims, kind) for dims, kind in table_shapes],
+            dma, dma((6,)),
             dma((4, n)), dma((4, n)), dma((4,)),
             dma((2, 2, rows)), dma((2, 2, rows)),
             dma((2, 2, n)), dma((2, 2, n)),
@@ -439,7 +481,7 @@
         ],
         compiler_params=pltpu.CompilerParams(
             collective_id=0, has_side_effects=True, vmem_limit_bytes=56 * 1024 * 1024),
-    )(*lists, queries, keys, values, out_grad)
+    )(queries, keys, values, out_grad, tile_mask)
 
 
 def solution(mesh):

time: 91.3 us -> 83.6 us (0.916)
  other arithmetic: 5.18 us -> 0 us
  Pallas kernels: 79.6 us -> 77.5 us
    select_n x6 -> x0, other arithmetic: 2.52 us -> none  [the longest x1 0.68 us: tables(): chosen = jnp.where(present, chosen, n + i[:, None])]
    pallas_call x1, Pallas kernels: 79.6 us -> 77.5 us  [body(): pl.pallas_call(functools.partial(kernel, rows, cols, slots, groups, frame...]
    reduce_sum x6 -> x0, other arithmetic: 1.08 us -> none  [the longest x1 0.38 us: tables(): chosen = jnp.sum(jnp.where(hit, t[None, None, :], 0), axis=2)]
where the time goes in v2:
time: 83.6 us; the launch traced here: 83.4 us
  Pallas kernels  77.5 us (93%)
  local copies, waits for them, and re-layouts  5.19 us (6%)
    pallas_call x1, Pallas kernels, body(): pl.pallas_call(functools.partial(kernel, rows, cols, slots, groups, frame...  77.5 us
    unnamed x10, local copies, waits for them, and re-layouts  5.19 us

profile of v2, /device:TPU:129, one launch (start us, length us, event | category | flops | bytes accessed | tf_op | source)
XLA Modules:
  0.0 83.4 jit_solution(10934621584787969832)
XLA Ops:
  0.6 77.5 %shard_map.84 = (bf16[1,128,2048]{2,1,0:T(8,128)(2,1)}, bf16[1,128,2048]{2,1,0:T(8,128)(2,1)}, bf16[1,128,2048]{2,1,0:T(8,128)(2,1)}, bf16[1,128,2048]{2,1,0:T(8,128)(2,1)}) custom-call(bf16[1,128,2048]{2,1,0:T(8,128)(2,1)} %q_in.1, bf16[1,128,2048]{2,1,0:T(8,128)(2,1)} %k_in.1, bf16[1,128,2048]{2,1,0:T(8,128)(2,1)} %v_in.1, bf16[1,128,2048]{2,1,0:T(8,128)(2,1)} %g_in.1, ...), custom_call_target="tpu_custom_call" | custom-call | tf_op jit(solution)/shard_map/pallas_call | solution.py:461
  78.2 0.0 copy-start.2
  78.2 1.9 %copy.13 = bf16[1,128,2048]{2,1,0:T(8,128)(2,1)} copy(bf16[1,128,2048]{2,1,0:T(8,128)(2,1)} %get-tuple-element.8) | data formatting | bytes 1048576
  80.1 0.0 copy-done.2
  80.1 0.0 copy-start.1
  80.1 0.8 copy.14
  80.9 0.4 copy-done.1
  81.4 0.0 copy-start
  81.4 0.8 copy.15
  82.1 0.4 copy-done
  82.6 0.8 copy.16
Async XLA Ops:
  78.2 2.0 %copy-start.2 = (bf16[1,128,2048]{2,1,0:T(8,128)(2,1)S(1)}, bf16[1,128,2048]{2,1,0:T(8,128)(2,1)}, u32[]{:S(2)}) copy-start(bf16[1,128,2048]{2,1,0:T(8,128)(2,1)} %get-tuple-element.9) | copy-start | bytes 1572868
  80.1 1.2 %copy-start.1 = (bf16[1,128,2048]{2,1,0:T(8,128)(2,1)S(1)}, bf16[1,128,2048]{2,1,0:T(8,128)(2,1)}, u32[]{:S(2)}) copy-start(bf16[1,128,2048]{2,1,0:T(8,128)(2,1)} %get-tuple-element.10) | copy-start | bytes 1572868
  81.4 1.2 %copy-start = (bf16[1,128,2048]{2,1,0:T(8,128)(2,1)S(1)}, bf16[1,128,2048]{2,1,0:T(8,128)(2,1)}, u32[]{:S(2)}) copy-start(bf16[1,128,2048]{2,1,0:T(8,128)(2,1)} %get-tuple-element.11) | copy-start | bytes 1572868

commit v3 on v2

--- a/solution.py
+++ b/solution.py
@@ -137,11 +137,18 @@
     for a in range(4):
         in_own(a).start()
 
-        def send(r, _, a=a):
+    def send(first, last, a):
+        def one(r, _):
             in_copy(a, peer(r, 1), me).start()
             return 0
 
-        lax.fori_loop(1, n, send, 0)
+        lax.fori_loop(first, last, one, 0)
+
+    send(1, n, 0)
+    send(1, n, 1)
+    for dr in range(rows):
+        for a in (2, 3):
+            send(max(1, dr * cols), (dr + 1) * cols, a)
 
     def halo_copy(a, side, chunk):
         ref = (k3, v3)[a]
@@ -372,14 +379,14 @@
 
     def neighbour_terms(a):
         def four(b, _):
+            tiles = [peer(b * BLOCK + u, -1) for u in range(BLOCK)]
             for side, send_if, _ in sides:
                 @pl.when(send_if)
                 def _(side=side):
-                    for u in range(BLOCK):
-                        i = b * BLOCK + u
+                    for i in tiles:
                         snd[side, a, i] = tile_of(a, i if side == 0 else 2 * n + i)
-                    for u in range(BLOCK):
-                        gr_copy(a, side, b * BLOCK + u).start()
+                    for i in tiles:
+                        gr_copy(a, side, i).start()
             return 0
 
         lax.fori_loop(0, n // BLOCK, four, 0)

time: 83.6 us -> 81.2 us (0.971); the launches traced: 83.4 us -> 80 us
  Pallas kernels: 77.5 us -> 74.2 us
    pallas_call x1, Pallas kernels: 77.5 us -> 74.2 us  [body(): pl.pallas_call(functools.partial(kernel, rows, cols, slots, groups, frame...]
where the time goes in v3:
time: 81.2 us; the launch traced here: 80 us
  Pallas kernels  74.2 us (91%)
  local copies, waits for them, and re-layouts  5.19 us (6%)
    pallas_call x1, Pallas kernels, body(): pl.pallas_call(functools.partial(kernel, rows, cols, slots, groups, frame...  74.2 us
    unnamed x10, local copies, waits for them, and re-layouts  5.19 us

profile of v3, /device:TPU:129, one launch (start us, length us, event | category | flops | bytes accessed | tf_op | source)
XLA Modules:
  0.0 80.0 jit_solution(18181708700637764563)
XLA Ops:
  0.6 74.2 %shard_map.84 = (bf16[1,128,2048]{2,1,0:T(8,128)(2,1)}, bf16[1,128,2048]{2,1,0:T(8,128)(2,1)}, bf16[1,128,2048]{2,1,0:T(8,128)(2,1)}, bf16[1,128,2048]{2,1,0:T(8,128)(2,1)}) custom-call(bf16[1,128,2048]{2,1,0:T(8,128)(2,1)} %q_in.1, bf16[1,128,2048]{2,1,0:T(8,128)(2,1)} %k_in.1, bf16[1,128,2048]{2,1,0:T(8,128)(2,1)} %v_in.1, bf16[1,128,2048]{2,1,0:T(8,128)(2,1)} %g_in.1, ...), custom_call_target="tpu_custom_call" | custom-call | tf_op jit(solution)/shard_map/pallas_call | solution.py:468
  74.8 0.0 copy-start.2
  74.8 1.9 %copy.13 = bf16[1,128,2048]{2,1,0:T(8,128)(2,1)} copy(bf16[1,128,2048]{2,1,0:T(8,128)(2,1)} %get-tuple-element.8) | data formatting | bytes 1048576
  76.8 0.0 copy-done.2
  76.8 0.0 copy-start.1
  76.8 0.8 copy.14
  77.6 0.4 copy-done.1
  78.0 0.0 copy-start
  78.0 0.8 copy.15
  78.8 0.4 copy-done
  79.2 0.8 copy.16
Async XLA Ops:
  74.8 2.0 %copy-start.2 = (bf16[1,128,2048]{2,1,0:T(8,128)(2,1)S(1)}, bf16[1,128,2048]{2,1,0:T(8,128)(2,1)}, u32[]{:S(2)}) copy-start(bf16[1,128,2048]{2,1,0:T(8,128)(2,1)} %get-tuple-element.9) | copy-start | bytes 1572868
  76.8 1.2 %copy-start.1 = (bf16[1,128,2048]{2,1,0:T(8,128)(2,1)S(1)}, bf16[1,128,2048]{2,1,0:T(8,128)(2,1)}, u32[]{:S(2)}) copy-start(bf16[1,128,2048]{2,1,0:T(8,128)(2,1)} %get-tuple-element.10) | copy-start | bytes 1572868
  78.0 1.2 %copy-start = (bf16[1,128,2048]{2,1,0:T(8,128)(2,1)S(1)}, bf16[1,128,2048]{2,1,0:T(8,128)(2,1)}, u32[]{:S(2)}) copy-start(bf16[1,128,2048]{2,1,0:T(8,128)(2,1)} %get-tuple-element.11) | copy-start | bytes 1572868

commit v4 on v3

--- a/solution.py
+++ b/solution.py
@@ -82,7 +82,7 @@
     rows, cols, slots, groups, frames,
     q_in, k_in, v_in, g_in, mask_in,
     o_out, dq_out, dk_out, dv_out,
-    k3, v3, qh, gh, sbuf, pst, dst, qt, gt, park, parv, ot, dqt, snd, rcv, dkt, dvt,
+    k3, v3, qh, gh, sbuf, row_dots, inverses, pst, dst, qt, gt, park, parv, ot, dqt, snd, rcv, dkt, dvt,
     mask, ci_v, gp_v, gq_v, last_v, bias_v, hold_v, ci, gp, gq, last, bias, hold, mask_sem, table_sem,
     in_send, in_recv, in_local, halo_send, halo_recv, gr_send, gr_recv, out_send, out_recv, out_local,
 ):
@@ -163,6 +163,38 @@
         )
 
     sides = ((0, has_prev, has_next), (1, has_next, has_prev))
+    zero_tile = jnp.zeros((HD, HD), jnp.bfloat16)
+    pst[n * slots] = zero_tile
+    dst[n * slots] = zero_tile
+    park[groups] = zero_tile
+    parv[groups] = zero_tile
+
+    @pl.when(jnp.logical_not(has_prev))
+    def _():
+        k3[0:n] = jnp.zeros((n, HD, HD), jnp.bfloat16)
+        v3[0:n] = jnp.zeros((n, HD, HD), jnp.bfloat16)
+        rcv[1] = jnp.zeros(rcv.shape[1:], jnp.bfloat16)
+
+    @pl.when(jnp.logical_not(has_next))
+    def _():
+        k3[2 * n : 3 * n] = jnp.zeros((n, HD, HD), jnp.bfloat16)
+        v3[2 * n : 3 * n] = jnp.zeros((n, HD, HD), jnp.bfloat16)
+        rcv[0] = jnp.zeros(rcv.shape[1:], jnp.bfloat16)
+
+    def pass_on(a):
+        in_own(a).wait()
+        for dr in range(rows):
+            for dc in range(cols):
+                r = dr * cols + dc
+                if r > 0:
+                    in_copy(a, peer(r, 1), peer(r, -1)).wait_recv()
+            chunk = lax.rem(my_row - dr + rows, rows)
+            for side, send_if, _ in sides:
+                @pl.when(send_if)
+                def _(side=side, chunk=chunk):
+                    halo_copy(a, side, chunk).start()
+
+    pass_on(0)
     mask_copy.wait()
     build_tables(mask, frame, slots, groups, (ci_v, gp_v, gq_v, last_v, bias_v, hold_v))
     moves = [
@@ -172,39 +204,9 @@
     ]
     for move in moves:
         move.start()
-    zero_tile = jnp.zeros((HD, HD), jnp.bfloat16)
-    pst[n * slots] = zero_tile
-    dst[n * slots] = zero_tile
-    park[groups] = zero_tile
-    parv[groups] = zero_tile
-
-    @pl.when(jnp.logical_not(has_prev))
-    def _():
-        k3[0:n] = jnp.zeros((n, HD, HD), jnp.bfloat16)
-        v3[0:n] = jnp.zeros((n, HD, HD), jnp.bfloat16)
-        rcv[1] = jnp.zeros(rcv.shape[1:], jnp.bfloat16)
-
-    @pl.when(jnp.logical_not(has_next))
-    def _():
-        k3[2 * n : 3 * n] = jnp.zeros((n, HD, HD), jnp.bfloat16)
-        v3[2 * n : 3 * n] = jnp.zeros((n, HD, HD), jnp.bfloat16)
-        rcv[0] = jnp.zeros(rcv.shape[1:], jnp.bfloat16)
-
+    pass_on(1)
     for move in moves:
         move.wait()
-
-    for a in range(2):
-        in_own(a).wait()
-        for dr in range(rows):
-            for dc in range(cols):
-                r = dr * cols + dc
-                if r > 0:
-                    in_copy(a, peer(r, 1), peer(r, -1)).wait_recv()
-            chunk = lax.rem(my_row - dr + rows, rows)
-            for side, send_if, _ in sides:
-                @pl.when(send_if)
-                def _(a=a, side=side, chunk=chunk):
-                    halo_copy(a, side, chunk).start()
 
     for a in range(2):
         for side, _, recv_if in sides:
@@ -243,13 +245,11 @@
         one, two = within(ci[i, 2 * jj], 3 * n), within(ci[i, 2 * jj + 1], 3 * n)
         return jnp.concatenate([ref[one], ref[two]], axis=0)
 
-    def query_phases(i, logits):
+    def score_phases(i, logits):
         held = {}
 
         def scores():
             q = qh[i]
-            gt[i] = gh[i].astype(jnp.float32).T.astype(jnp.bfloat16)
-            qt[i] = q.astype(jnp.float32).T.astype(jnp.bfloat16)
             top = jnp.full((HD, HD), NEG, jnp.float32)
             for jj in range(half):
                 s = dot_nt(q, pair_of(k3, i, jj)) * (scale * LOG2E)
@@ -266,40 +266,56 @@
             total = jnp.zeros((HD, HD), jnp.float32)
             o = jnp.zeros((HD, HD), jnp.float32)
             for jj in range(half):
-                at = slice(jj * 2 * HD, (jj + 1) * 2 * HD)
-                p = jnp.exp2(logits[:, at] - highest)
-                logits[:, at] = p
+                p = jnp.exp2(logits[:, jj * 2 * HD : (jj + 1) * 2 * HD] - highest)
                 total = total + (p[:, :HD] + p[:, HD:])
-                o = o + dot_nn(p.astype(jnp.bfloat16), pair_of(v3, i, jj))
+                pb = p.astype(jnp.bfloat16)
+                base = i * slots + 2 * jj
+                pst[base] = pb[:, :HD]
+                pst[base + 1] = pb[:, HD:]
+                o = o + dot_nn(pb, pair_of(v3, i, jj))
                 yield
             inv = 1.0 / jnp.sum(total, axis=1, keepdims=True)
             ob = (o * inv).astype(jnp.bfloat16)
             ot[i] = ob
-            held["inv"] = inv
-            held["row_dot"] = jnp.sum(
-                gh[i].astype(jnp.float32) * ob.astype(jnp.float32), axis=1, keepdims=True)
-
-        def gradients():
-            g, inv, row_dot = gh[i], held["inv"], held["row_dot"]
-            dq = jnp.zeros((HD, HD), jnp.float32)
-            for jj in range(half):
-                at = slice(jj * 2 * HD, (jj + 1) * 2 * HD)
-                p = logits[:, at] * inv
-                dp = dot_nt(g, pair_of(v3, i, jj))
-                ds = (p * (dp - row_dot)).astype(jnp.bfloat16)
-                pb = p.astype(jnp.bfloat16)
-                dq = dq + dot_nn(ds, pair_of(k3, i, jj))
-                base = i * slots + 2 * jj
-                pst[base] = pb[:, :HD]
-                pst[base + 1] = pb[:, HD:]
-                dst[base] = ds[:, :HD]
-                dst[base + 1] = ds[:, HD:]
-                yield
-            dqt[i] = (dq * scale).astype(jnp.bfloat16)
-
-        return scores, output, gradients
-
-    def query_block(b, _):
+            g = gh[i].astype(jnp.float32)
+            row_dot = jnp.sum(g * ob.astype(jnp.float32), axis=1, keepdims=True)
+            gt[i] = (g * inv).T.astype(jnp.bfloat16)
+            qt[i] = (qh[i].astype(jnp.float32) * inv).T.astype(jnp.bfloat16)
+            row_dots[i] = jnp.broadcast_to(row_dot, (HD, HD))
+            inverses[i] = jnp.broadcast_to(inv, (HD, HD))
+
+        return scores, output
+
+    def gradients(i):
+        g, row_dot = gh[i], row_dots[i]
+        dq = jnp.zeros((HD, HD), jnp.float32)
+        for jj in range(half):
+            dp = dot_nt(g, pair_of(v3, i, jj))
+            base = i * slots + 2 * jj
+            ds0 = (pst[base].astype(jnp.float32) * (dp[:, :HD] - row_dot)).astype(jnp.bfloat16)
+            ds1 = (pst[base + 1].astype(jnp.float32) * (dp[:, HD:] - row_dot)).astype(jnp.bfloat16)
+            dst[base] = ds0
+            dst[base + 1] = ds1
+            dq = dq + dot_nn(jnp.concatenate([ds0, ds1], axis=1), pair_of(k3, i, jj))
+            yield
+        dqt[i] = (dq * (inverses[i] * scale)).astype(jnp.bfloat16)
+
+    def leave_block(a, b, tiles):
+        for u in range(BLOCK):
+
+            def leave(u=u):
+                out_copy(a, tiles[u], me).start()
+
+            if u > 0:
+                leave()
+            else:
+                pl.when(b > 0)(leave)
+
+                @pl.when(b == 0)
+                def _():
+                    out_own(a).start()
+
+    def score_block(b, _):
         tiles = [peer(b * BLOCK + u, -1) for u in range(BLOCK)]
         for u in range(BLOCK):
             r = b * BLOCK + u
@@ -318,33 +334,20 @@
                     for a in (2, 3):
                         in_own(a).wait()
 
-        steps = [query_phases(tiles[u], sbuf.at[u]) for u in range(BLOCK)]
+        steps = [score_phases(tiles[u], sbuf.at[u]) for u in range(BLOCK)]
         together(steps[0][0]())
         for u in range(BLOCK):
-            if u + 1 < BLOCK:
-                together(steps[u][1](), steps[u + 1][0]())
-                together(steps[u][2]())
-            else:
-                together(steps[u][1]())
-                together(steps[u][2]())
-        for u in range(BLOCK):
-
-            def leave(u=u):
-                for a in (0, 1):
-                    out_copy(a, tiles[u], me).start()
-
-            if u > 0:
-                leave()
-            else:
-                pl.when(b > 0)(leave)
-
-                @pl.when(b == 0)
-                def _():
-                    for a in (0, 1):
-                        out_own(a).start()
+            after = [steps[u + 1][0]()] if u + 1 < BLOCK else []
+            together(steps[u][1](), *after)
+        leave_block(0, b, tiles)
         return 0
 
-    lax.fori_loop(0, n // BLOCK, query_block, 0)
+    def gradient_block(b, _):
+        tiles = [peer(b * BLOCK + u, -1) for u in range(BLOCK)]
+        for u in range(0, BLOCK, 2):
+            together(gradients(tiles[u]), gradients(tiles[u + 1]))
+        leave_block(1, b, tiles)
+        return 0
 
     def key_side(a):
         left, right, par = ((qt, dst, park), (gt, pst, parv))[a]
@@ -403,28 +406,18 @@
                 tot = tile_of(a, n + i).astype(jnp.float32)
                 tot = tot + rcv[0, a, i].astype(jnp.float32) + rcv[1, a, i].astype(jnp.float32)
                 (dkt, dvt)[a][i] = tot.astype(jnp.bfloat16)
-            for u, i in enumerate(tiles):
-
-                def leave(i=i):
-                    out_copy(2 + a, i, me).start()
-
-                if u > 0:
-                    leave()
-                else:
-                    pl.when(b > 0)(leave)
-
-                    @pl.when(b == 0)
-                    def _():
-                        out_own(2 + a).start()
+            leave_block(2 + a, b, tiles)
             return 0
 
         lax.fori_loop(0, n // BLOCK, four, 0)
 
+    lax.fori_loop(0, n // BLOCK, score_block, 0)
     key_side(1)
     neighbour_terms(1)
+    lax.fori_loop(0, n // BLOCK, gradient_block, 0)
+    finish(1)
     key_side(0)
     neighbour_terms(0)
-    finish(1)
     finish(0)
 
     for a in range(4):
@@ -473,6 +466,7 @@
         scratch_shapes=[
             tile(3 * n), tile(3 * n), tile(n), tile(n),
             pltpu.VMEM((BLOCK, HD, slots * HD), jnp.float32),
+            pltpu.VMEM((n, HD, HD), jnp.float32), pltpu.VMEM((n, HD, HD), jnp.float32),
             tile(n * slots + 1), tile(n * slots + 1),
             tile(n), tile(n),
             tile(groups + 1), tile(groups + 1),

time: 81.2 us -> 82.4 us (1.015)
  Pallas kernels: 74.2 us -> 75.9 us
    pallas_call x1, Pallas kernels: 74.2 us -> 75.9 us  [body(): pl.pallas_call(functools.partial(kernel, rows, cols, slots, groups, frame...]
where the time goes in v4:
time: 82.4 us; the launch traced here: 81.7 us
  Pallas kernels  75.9 us (92%)
  local copies, waits for them, and re-layouts  5.19 us (6%)
    pallas_call x1, Pallas kernels, body(): pl.pallas_call(functools.partial(kernel, rows, cols, slots, groups, frame...  75.9 us
    unnamed x10, local copies, waits for them, and re-layouts  5.19 us

profile of v4, /device:TPU:129, one launch (start us, length us, event | category | flops | bytes accessed | tf_op | source)
XLA Modules:
  0.0 81.7 jit_solution(8433655431650852461)
XLA Ops:
  0.6 75.9 %shard_map.84 = (bf16[1,128,2048]{2,1,0:T(8,128)(2,1)}, bf16[1,128,2048]{2,1,0:T(8,128)(2,1)}, bf16[1,128,2048]{2,1,0:T(8,128)(2,1)}, bf16[1,128,2048]{2,1,0:T(8,128)(2,1)}) custom-call(bf16[1,128,2048]{2,1,0:T(8,128)(2,1)} %q_in.1, bf16[1,128,2048]{2,1,0:T(8,128)(2,1)} %k_in.1, bf16[1,128,2048]{2,1,0:T(8,128)(2,1)} %v_in.1, bf16[1,128,2048]{2,1,0:T(8,128)(2,1)} %g_in.1, ...), custom_call_target="tpu_custom_call" | custom-call | tf_op jit(solution)/shard_map/pallas_call | solution.py:461
  76.5 0.0 copy-start.2
  76.5 1.9 %copy.13 = bf16[1,128,2048]{2,1,0:T(8,128)(2,1)} copy(bf16[1,128,2048]{2,1,0:T(8,128)(2,1)} %get-tuple-element.8) | data formatting | bytes 1048576
  78.5 0.0 copy-done.2
  78.5 0.0 copy-start.1
  78.5 0.8 copy.14
  79.3 0.4 copy-done.1
  79.7 0.0 copy-start
  79.7 0.8 copy.15
  80.5 0.4 copy-done
  81.0 0.8 copy.16
Async XLA Ops:
  76.5 2.0 %copy-start.2 = (bf16[1,128,2048]{2,1,0:T(8,128)(2,1)S(1)}, bf16[1,128,2048]{2,1,0:T(8,128)(2,1)}, u32[]{:S(2)}) copy-start(bf16[1,128,2048]{2,1,0:T(8,128)(2,1)} %get-tuple-element.9) | copy-start | bytes 1572868
  78.5 1.2 %copy-start.1 = (bf16[1,128,2048]{2,1,0:T(8,128)(2,1)S(1)}, bf16[1,128,2048]{2,1,0:T(8,128)(2,1)}, u32[]{:S(2)}) copy-start(bf16[1,128,2048]{2,1,0:T(8,128)(2,1)} %get-tuple-element.10) | copy-start | bytes 1572868
  79.7 1.2 %copy-start = (bf16[1,128,2048]{2,1,0:T(8,128)(2,1)S(1)}, bf16[1,128,2048]{2,1,0:T(8,128)(2,1)}, u32[]{:S(2)}) copy-start(bf16[1,128,2048]{2,1,0:T(8,128)(2,1)} %get-tuple-element.11) | copy-start | bytes 1572868
